TPU v7x, 256 devices: a whole 4x4x8 slice. The times are simulated.
256 devices in a mesh: ctx: 64 (over x, z, core), fsdp: 4 (over y).
Axes of the slice: x: 4, y: 4, z: 8, core: 2. Of those that a mesh axis runs over, the one named last changes fastest.
Arguments:
- acts: bfloat16 [131072, 4096], P(('ctx', 'fsdp')), may hold values from -64 to 64
- queries: bfloat16 [131072, 2048], P(('ctx', 'fsdp')), may hold values from -120 to 120
- kv_weight: bfloat16 [4096, 4, 2, 128], P(None, 'fsdp'), may hold values from -1 to 1
- rand_blocks: int32 [1024, 3], replicated, may hold values from 0 to 1023, as said below
Outputs:
- attended: bfloat16 [131072, 2048], P(('ctx', 'fsdp'))
Inputs may be any that keep to these rules, and one draw needn't show every extreme that they name: `rand_blocks`: call the 16 consecutive blocks of one index of ctx a context shard. Among the 48 entries of the rows of one context shard, the blocks of any one context shard are named at most 1 times in all, and some context shard is named exactly 1 times.
All inputs are finite; a program needn't handle non-finite values.
Results may differ from a plain program's by a relative error of at most 0.0086.
Values may be sent and summed in bfloat16 or wider, within the bound.
A program may use at most 128 MiB of HBM per device.

v0:
```python
import math

import jax
import jax.numpy as jnp
from jax import lax
from jax.sharding import PartitionSpec as P

BLOCK = 128
GLOBAL = 2
RAND = 3


def with_halo(value, sides, width):
    for axis, dim in sides:
        size, length = (lax.axis_size(axis), value.shape[dim])
        up = [(i, (i + 1) % size) for i in range(size)]
        down = [(j, i) for i, j in up]
        last = lax.slice_in_dim(value, length - width, length, axis=dim)
        initial = lax.slice_in_dim(value, 0, width, axis=dim)
        before = lax.ppermute(last, axis, up)
        after = lax.ppermute(initial, axis, down)
        value = jnp.concatenate([before, value, after], axis=dim)
    return value


def broadcast(block, axis, holder):
    block = jnp.where(lax.axis_index(axis) == holder, block, jnp.zeros_like(block))
    return lax.psum(block, axis)


def shards(acts, queries, kv_weight, rand_blocks):
    ctx_count = lax.axis_size("ctx")
    fsdp_count = lax.axis_size("fsdp")
    tok_rows = acts.shape[0]
    model_width = acts.shape[1]
    kv_heads = kv_weight.shape[1]
    head_size = kv_weight.shape[3]
    shard_rows = tok_rows * fsdp_count
    shard_blocks = shard_rows // BLOCK
    row_width = kv_heads * 2 * head_size
    flat_weight = kv_weight.reshape(model_width, row_width)
    projected = jnp.dot(
        lax.all_gather(acts, "fsdp", axis=0, tiled=True),
        flat_weight,
        preferred_element_type=jnp.float32,
    ).astype(jnp.bfloat16)
    query_heads = lax.all_to_all(queries, "fsdp", split_axis=1, concat_axis=0, tiled=True)
    padded = with_halo(projected, (("ctx", 0),), BLOCK)
    padded = padded.reshape(shard_blocks + 2, BLOCK * row_width)
    leading = broadcast(projected[: GLOBAL * BLOCK], "ctx", 0)
    leading = leading.reshape(GLOBAL, BLOCK * row_width)
    position = lax.axis_index("ctx")
    capacity = (RAND * shard_blocks + ctx_count - 1) // ctx_count
    entries = shard_blocks * RAND
    requests = rand_blocks.reshape(ctx_count, entries)
    from_me = requests // shard_blocks == position
    slot_rank = jnp.cumsum(from_me.astype(jnp.int32), axis=1) - 1
    slot_ids = jnp.arange(capacity, dtype=jnp.int32)
    slot_hit = from_me[:, :, None] & (slot_rank[:, :, None] == slot_ids[None, None, :])
    chosen = jnp.sum(jnp.where(slot_hit, (requests % shard_blocks)[:, :, None], 0), axis=1)
    block_rows = projected.reshape(shard_blocks, BLOCK * row_width)
    outgoing = block_rows[chosen.reshape(-1)].reshape(ctx_count, capacity, BLOCK * row_width)
    incoming = lax.all_to_all(outgoing, "ctx", split_axis=0, concat_axis=0, tiled=True)
    wanted = lax.dynamic_slice_in_dim(requests, position, 1, 0)[0]
    source = wanted // shard_blocks
    same_source = source[:, None] == source[None, :]
    entry_ids = jnp.arange(entries, dtype=jnp.int32)
    before = entry_ids[None, :] < entry_ids[:, None]
    arrival = jnp.sum((same_source & before).astype(jnp.int32), axis=1)
    pool = jnp.concatenate(
        [padded, leading, incoming.reshape(ctx_count * capacity, BLOCK * row_width)], axis=0
    )
    local_ids = jnp.arange(shard_blocks, dtype=jnp.int32)
    window_ids = jnp.stack([local_ids, local_ids + 1, local_ids + 2], axis=1)
    global_ids = jnp.broadcast_to(
        shard_blocks + 2 + jnp.arange(GLOBAL, dtype=jnp.int32)[None, :], (shard_blocks, GLOBAL)
    )
    random_ids = (shard_blocks + 2 + GLOBAL + source * capacity + arrival).reshape(
        shard_blocks, RAND
    )
    list_ids = jnp.concatenate([window_ids, global_ids, random_ids], axis=1)
    list_len = list_ids.shape[1]
    key_count = list_len * BLOCK
    group_size = query_heads.shape[1] // (kv_heads * head_size)
    query_rows = query_heads.reshape(shard_blocks, BLOCK, kv_heads, group_size, head_size)
    per_step = 2
    step_count = shard_blocks // per_step
    scale = 1.0 / math.sqrt(head_size)

    def attend_group(operands):
        query_part, id_part = operands
        listed = pool[id_part.reshape(-1)].reshape(per_step, key_count, kv_heads, 2, head_size)
        key_part = listed[:, :, :, 0, :]
        value_part = listed[:, :, :, 1, :]
        scores = (
            jnp.einsum(
                "bqhgd,bkhd->bhgqk", query_part, key_part, preferred_element_type=jnp.float32
            )
            * scale
        )
        largest = jnp.max(scores, axis=-1, keepdims=True)
        weights = jnp.exp(scores - largest)
        probs = (weights / jnp.sum(weights, axis=-1, keepdims=True)).astype(jnp.bfloat16)
        result = jnp.einsum(
            "bhgqk,bkhd->bqhgd", probs, value_part, preferred_element_type=jnp.float32
        )
        return result.astype(jnp.bfloat16)

    attended = lax.map(
        attend_group,
        (
            query_rows.reshape(step_count, per_step, BLOCK, kv_heads, group_size, head_size),
            list_ids.reshape(step_count, per_step, list_len),
        ),
    )
    attended = attended.reshape(shard_rows, kv_heads * group_size * head_size)
    return lax.all_to_all(attended, "fsdp", split_axis=0, concat_axis=1, tiled=True)


def solution(mesh):
    placed = (P(("ctx", "fsdp"), None), P(("ctx", "fsdp"), None), P(None, "fsdp", None, None), P())
    return jax.shard_map(
        shards, mesh=mesh, in_specs=placed, out_specs=P(("ctx", "fsdp"), None), check_vma=False
    )
```

profile of v0, /device:TPU:1, one launch (start us, length us, event | category | flops | bytes accessed | tf_op | source)
XLA Modules:
  0.0 607.7 jit_solution(9314805163690859546)
XLA Ops:
  9.6 5.0 all-to-all-start.1
  17.0 159.7 %all-gather.2.cloned.1.call-done = bf16[2048,4096]{1,0:T(8,128)(2,1)} async-done(((bf16[512,4096]{1,0:T(8,128)(2,1)}), bf16[2048,4096]{1,0:T(8,128)(2,1)}) %all-gather.2.cloned.1.call-update) | async-done | bytes 16777232 | tf_op jit(solution)/shard_map/all_gather | solution.py:43
  176.7 12.1 %convolution_convert_fusion = bf16[2048,256]{1,0:T(8,128)(2,1)} fusion(bf16[2048,4096]{1,0:T(8,128)(2,1)} %all-gather.2.cloned.1.call-done, bf16[512,8,2,128]{3,2,1,0:T(2,128)(2,1)} %bitcast.112), kind=kOutput, calls=%fused_computation.25 | convolution fusion | flops 4295491584 | bytes 19922944 | tf_op jit(solution)/shard_map/dot_general | solution.py:42
  190.3 5.2 gather_fusion.1
  196.0 6.7 %reduce.9 = bf16[64,32768]{1,0:T(8,128)(2,1)} reduce(bf16[64,1,32768]{2,0,1:T(8,128)(2,1)} %bitcast.105, bf16[]{:T(256)} %broadcast.262), dimensions={1}, to_apply=%copy.104.reduce_sub_computation | reduce | bytes 8388610 | tf_op jit(solution)/shard_map/reshape | solution.py:62
  202.6 7.8 %reshape.222 = bf16[64,2,16384]{2,1,0:T(2,128)(2,1)} reshape(bf16[64,32768]{1,0:T(8,128)(2,1)} %reduce.9) | data formatting | bytes 8388608
  210.5 12.1 %all-to-all-start = ((bf16[64,2,16384]{2,1,0:T(2,128)(2,1)}), bf16[64,2,16384]{2,1,0:T(2,128)(2,1)}, u32[]{:S(2)}, u32[]{:S(2)}) async-start(bf16[64,2,16384]{2,1,0:T(2,128)(2,1)} %reshape.222), calls=%async_computation | async-start | bytes 8388608 | tf_op jit(solution)/shard_map/all_to_all | solution.py:63
  228.2 85.2 %collective-permute-done = bf16[128,256]{1,0:T(8,128)(2,1)S(1)} collective-permute-done((bf16[128,256]{1,0:T(8,128)(2,1)S(1)}, bf16[128,256]{1,0:T(8,128)(2,1)S(1)}, u32[]{:S(2)}, u32[]{:S(2)}) %collective-permute-start) | collective-permute-done | bytes 65568 | tf_op jit(solution)/shard_map/ppermute | solution.py:20
  319.5 19.8 %reshape.223 = bf16[64,1,32768]{2,1,0:T(2,128)(2,1)} reshape(bf16[64,2,16384]{2,1,0:T(2,128)(2,1)} %all-to-all-done) | data formatting | bytes 8388608
  339.3 9.9 %copy.143 = bf16[64,1,32768]{2,0,1:T(8,128)(2,1)} copy(bf16[64,1,32768]{2,1,0:T(2,128)(2,1)} %reshape.223) | data formatting | bytes 8388608
  349.2 68.8 %all-reduce.2.cloned.1.call-done = bf16[2,32768]{1,0:T(2,128)(2,1)} async-done(((bf16[2,32768]{1,0:T(2,128)(2,1)}), bf16[2,32768]{1,0:T(2,128)(2,1)}) %all-reduce.2.cloned.1.call-update) | async-done | bytes 131088 | tf_op jit(solution)/shard_map/psum | solution.py:28
  418.0 6.3 %pad_maximum_fusion = bf16[84,32768]{1,0:T(8,128)(2,1)} fusion(bf16[64,32768]{1,0:T(8,128)(2,1)} %bitcast.106, bf16[2,32768]{1,0:T(2,128)(2,1)} %all-reduce.2.cloned.1.call-done, bf16[18,32768]{1,0:T(8,128)(2,1)S(1)} %reshape.192), kind=kLoop, calls=%fused_computation.23 | loop fusion | flops 16515072 | bytes 11010048 | tf_op jit(solution)/shard_map/concatenate | solution.py:70
  424.3 137.9 %while.10 = (s32[]{:T(128)}, bf16[8,2,128,1,4,128]{5,4,2,1,0,3:T(4,128)(2,1)}, s32[8,2,8]{2,1,0:T(2,128)S(1)}, bf16[84,32768]{1,0:T(8,128)(2,1)}, bf16[8,2,128,1,4,128]{5,4,2,1,0,3:T(4,128)(2,1)}, /*index=5*/s32[]{:T(128)}) while((s32[]{:T(128)}, bf16[8,2,128,1,4,128]{5,4,2,1,0,3:T(4,128)(2,1)}, s32[8,2,8]{2,1,0:T(2,128)S(1)}, ...), condition=%wide.region_8.9_spmd, body=%wide.region_5.8_spmd.sunk | while | flops 546438208 | bytes 39871592 | solution.py:109
  424.4 5.5 gather_fusion
  437.4 3.2 fusion.43
  441.6 5.5 gather_fusion
  454.6 3.2 fusion.43
  458.9 5.5 gather_fusion
  476.1 5.5 gather_fusion
  493.4 5.5 gather_fusion
  510.6 5.5 gather_fusion
  527.8 5.5 gather_fusion
  545.1 5.5 gather_fusion
  565.0 30.7 %all_to_all.40 = bf16[4,512,512]{2,1,0:T(8,128)(2,1)} all-to-all(bf16[4,512,512]{2,1,0:T(8,128)(2,1)S(1)} %all_to_all.33), channel_id=1, replica_groups=mesh['ctx'=64,'fsdp'=4] {'fsdp'}, dimensions={0} | all-to-all | bytes 4194304 | tf_op jit(solution)/shard_map/all_to_all | solution.py:117
  (174 shorter events, 114.2 us)
Async XLA Ops:
  6.5 1.6 copy-start.2
  6.5 170.1 %all-gather.2.cloned.1.call-start = ((), (), s32[]{:S(2)}) async-start(), calls=%async_computation.3 | async-start | bytes 20971520 | tf_op jit(solution)/shard_map/all_gather | solution.py:43
  8.1 6.5 %copy-start.3 = (s32[1024,3]{0,1:T(4,128)S(1)}, s32[1024,3]{0,1:T(4,128)}, u32[]{:S(2)}) copy-start(s32[1024,3]{0,1:T(4,128)} %param.9) | copy-start | bytes 36868
  9.6 200.8 %all-to-all-start.1 = ((bf16[512,4,512]{2,0,1:T(8,128)(2,1)}), bf16[512,4,512]{2,0,1:T(8,128)(2,1)S(1)}, u32[]{:S(2)}, u32[]{:S(2)}) async-start(bf16[512,4,512]{2,0,1:T(8,128)(2,1)} %bitcast.108), calls=%async_computation.1 | async-start | bytes 4194304 | tf_op jit(solution)/shard_map/all_to_all | solution.py:47
  210.5 109.1 %all-to-all-start = ((bf16[64,2,16384]{2,1,0:T(2,128)(2,1)}), bf16[64,2,16384]{2,1,0:T(2,128)(2,1)}, u32[]{:S(2)}, u32[]{:S(2)}) async-start(bf16[64,2,16384]{2,1,0:T(2,128)(2,1)} %reshape.222), calls=%async_computation | async-start | bytes 8388608 | tf_op jit(solution)/shard_map/all_to_all | solution.py:63
  222.6 3.1 copy-start.1
  222.6 195.4 %all-reduce.2.cloned.1.call-start = ((), (), s32[]{:S(2)}) async-start(), calls=%async_computation.4 | async-start | bytes 262144 | tf_op jit(solution)/shard_map/psum | solution.py:28
  225.7 87.6 %collective-permute-start = (bf16[128,256]{1,0:T(8,128)(2,1)S(1)}, bf16[128,256]{1,0:T(8,128)(2,1)S(1)}, u32[]{:S(2)}, u32[]{:S(2)}) collective-permute-start(bf16[128,256]{1,0:T(8,128)(2,1)S(1)} %get-tuple-element.77), channel_id=1, source_target_pairs={{0,4},{4,8},{8,12},{12,16},{16,20},{20,24},{24,28},{28,32},{32,36}... | collective-permute-start | bytes 196616 | tf_op jit(solution)/shard_map/ppermute | solution.py:20
  227.4 88.9 %collective-permute-start.1 = (bf16[128,256]{1,0:T(8,128)(2,1)S(1)}, bf16[128,256]{1,0:T(8,128)(2,1)S(1)}, u32[]{:S(2)}, u32[]{:S(2)}) collective-permute-start(bf16[128,256]{1,0:T(8,128)(2,1)S(1)} %get-tuple-element.78), channel_id=1, source_target_pairs={{4,0},{8,4},{12,8},{16,12},{20,16},{24,20},{28,24},{32,28},{36,32}... | collective-permute-start | bytes 196616 | tf_op jit(solution)/shard_map/ppermute | solution.py:21
  433.9 2.0 copy-start
  451.2 2.0 copy-start
  468.4 2.0 copy-start
  485.7 2.0 copy-start
  502.9 2.0 copy-start
  520.2 2.0 copy-start
  537.4 2.0 copy-start
  554.6 2.0 copy-start
Sparse Core Ops, SparseCore 0:
  9.2 167.4 all-gather.1
  228.3 189.6 all-reduce.1
where the time goes:
time: 610 us; the launch traced here: 608 us
  waiting for transfers between devices  320 us (52%)
  local copies, waits for them, and re-layouts  161 us (26%)
  matrix products  43.1 us (7%)
  blocking collectives  30.7 us (5%)
  other arithmetic  20.1 us (3%)
  starting transfers between devices  18.9 us (3%)
  between operations  13.6 us (2%)
    all_gather x1, waiting for transfers between devices, shards(): lax.all_gather(acts, 'fsdp', axis=0, tiled=True)  160 us
    ppermute x1, waiting for transfers between devices, with_halo(): before = lax.ppermute(last, axis, up)  85.2 us
    psum x1, waiting for transfers between devices, broadcast(): return lax.psum(block, axis)  68.8 us
    gather x8, local copies, waits for them, and re-layouts, attend_group(): pool[id_part.reshape(-1)]  43.8 us
    unnamed x10, local copies, waits for them, and re-layouts  38.6 us
    all_to_all x1, blocking collectives, shards(): lax.all_to_all(attended, 'fsdp', split_axis=0, concat_axis=1, tiled=True)  30.7 us
    dot_general x8, matrix products, attend_group(): jnp.einsum('bhgqk,bkhd->bqhgd', probs, value_part, preferred_element_type...  25.3 us
    while x24, local copies, waits for them, and re-layouts  21.5 us
  transfers between devices with their start and end apart: 6, of which 5 were waited for; matrix products, arithmetic and copies ran while one was open for 12% of the time, Pallas kernels for 0%

commit v1 on v0

v1 whole, which is shorter than its diff:
```python
import math

import jax
import jax.numpy as jnp
from jax import lax
from jax.experimental import pallas as pl
from jax.experimental.pallas import tpu as pltpu
from jax.sharding import PartitionSpec as P

BLOCK = 128
RAND = 3
NX, NZ, NY = 4, 8, 4
N_CTX = NX * NZ * 2
SHARD = 16
HEAD = 128
MODEL = 4096
TOK = 512
GROUP = 4
ROW = 2 * HEAD
QCOL = GROUP * HEAD
QUARTER = MODEL // 4
SUB = QUARTER // 4
SLOTS = 59
EXP2_SCALE = math.log2(math.e) / math.sqrt(HEAD)
NT = (((1,), (1,)), ((), ()))


def kernel(
    table, rand, acts, queries, weight, out,
    acts_v, wbuf, kv_send, kv, kvw, glob, before1, after1, before2, after2,
    stage, pool, qx, acc, top, total, outbox,
    loc, wy_s, wy_r, wd_s, wd_r, wx_s, wx_r, kv_s, kv_r, q_s, q_r,
    m_s, m_r, st_s, pool_r, halo_s, halo_r, g_s, g_r, out_s, out_r,
):
    c = lax.axis_index("ctx")
    y = lax.axis_index("fsdp")
    x = c // (2 * NZ)
    z = (c // 2) % NZ
    k = c % 2
    parity = (x + z) % 2

    def at(dx, dz, dk):
        return (((x + dx) % NX) * NZ + (z + dz) % NZ) * 2 + (k + dk) % 2

    def remote(src, dst, send, recv, ctx, head):
        return pltpu.make_async_remote_copy(
            src_ref=src, dst_ref=dst, send_sem=send, recv_sem=recv,
            device_id=(ctx, head), device_id_type=pl.DeviceIdType.MESH,
        )

    def peer(off):
        return (y + off) % NY

    sends = []

    def go(copy):
        copy.start()
        sends.append(copy)

    mine = (parity * 2 + k) * QUARTER
    other = ((1 - parity) * 2 + k) * QUARTER
    whole = pl.ds(mine, QUARTER)
    first = pl.ds(mine, QUARTER // 2)
    second = pl.ds(mine + QUARTER // 2, QUARTER // 2)
    for n, off in enumerate((1, 3)):
        go(remote(weight.at[whole], wbuf.at[y, whole], wy_s.at[n], wy_r.at[n], c, peer(off)))
    acts_in = pltpu.make_async_copy(acts, acts_v, loc.at[0])
    acts_in.start()
    own_w = pltpu.make_async_copy(weight, wbuf.at[y], loc.at[1])
    own_w.start()
    own_q = pltpu.make_async_copy(
        queries.at[:, pl.ds(pl.multiple_of(y * QCOL, QCOL), QCOL)],
        qx.at[pl.ds(y * TOK, TOK)], loc.at[2],
    )
    own_q.start()
    acts_in.wait()
    own_w.wait()

    def project(head, dest, lead):
        def tile(t, _):
            rows = pl.ds(t * 256, 256)
            total_ = jnp.dot(acts_v[rows, 0:1024], wbuf[head, 0:1024],
                             preferred_element_type=jnp.float32)
            for u in range(1, 4):
                total_ += jnp.dot(acts_v[rows, u * 1024:(u + 1) * 1024],
                                  wbuf[head, u * 1024:(u + 1) * 1024],
                                  preferred_element_type=jnp.float32)
            dest[pl.ds(lead + t * 2, 2)] = total_.astype(jnp.bfloat16).reshape(2, BLOCK, ROW)
            return 0
        lax.fori_loop(0, 2, tile, 0)

    project(y, kv, y * 4)

    def multicast(n, head):
        rows = pl.ds(head * 4, 4)
        go(remote(kv.at[rows], before1.at[rows], m_s.at[0, n], m_r.at[0, n], at(0, 1, 0), y))
        go(remote(kv.at[rows], after1.at[rows], m_s.at[1, n], m_r.at[1, n], at(0, -1 + NZ, 0), y))

    def spread(n, off):
        head = peer(off)
        go(remote(wbuf.at[head, whole], wbuf.at[head, whole], wd_s.at[0, n], wd_r.at[0, n],
                  at(0, 0, 1), y))
        for j, (dx, dz) in enumerate(((1, 0), (NX - 1, 0), (0, 1), (0, NZ - 1))):
            rows = pl.ds(mine + j * SUB, SUB)
            go(remote(wbuf.at[head, rows], wbuf.at[head, rows], wx_s.at[n, j], wx_r.at[n, j],
                      at(dx, dz, 0), y))

    def landed(view, send, recv):
        remote(view, view, send, recv, at(0, 0, 1), y).wait_recv()

    landed(wbuf.at[peer(3), whole], wy_s.at[0], wy_r.at[0])
    go(remote(wbuf.at[peer(3), first], wbuf.at[peer(3), first], wy_s.at[2], wy_r.at[2], c, peer(1)))
    landed(wbuf.at[peer(1), whole], wy_s.at[1], wy_r.at[1])
    go(remote(wbuf.at[peer(1), second], wbuf.at[peer(1), second], wy_s.at[3], wy_r.at[3], c, peer(3)))
    spread(0, 1)
    spread(1, 3)
    multicast(0, y)
    landed(wbuf.at[peer(2), first], wy_s.at[2], wy_r.at[2])
    landed(wbuf.at[peer(2), second], wy_s.at[3], wy_r.at[3])
    spread(2, 2)

    offs = (1, 3, 2)
    far = pl.ds(other, QUARTER)
    sib_mine = pl.ds((parity * 2 + 1 - k) * QUARTER, QUARTER)
    sib_other = pl.ds(((1 - parity) * 2 + 1 - k) * QUARTER, QUARTER)
    for n, off in enumerate(offs):
        head = peer(off)
        for j in range(4):
            landed(wbuf.at[head, pl.ds(other + j * SUB, SUB)], wx_s.at[n, j], wx_r.at[n, j])
        go(remote(wbuf.at[head, far], wbuf.at[head, far], wd_s.at[1, n], wd_r.at[1, n],
                  at(0, 0, 1), y))
        landed(wbuf.at[head, sib_mine], wd_s.at[0, n], wd_r.at[0, n])
        landed(wbuf.at[head, sib_other], wd_s.at[1, n], wd_r.at[1, n])
        project(head, kv_send.at[n], 0)
        go(remote(kv_send.at[n], kv.at[pl.ds(y * 4, 4)], kv_s.at[n], kv_r.at[n], c, head))

    for n, off in enumerate(offs):
        head = peer(NY - off)
        landed(kv.at[pl.ds(head * 4, 4)], kv_s.at[n], kv_r.at[n])
        multicast(n + 1, head)

    go(remote(kv.at[SHARD - 1], kvw.at[0], halo_s.at[0], halo_r.at[0], (c + 1) % N_CTX, y))
    go(remote(kv.at[0], kvw.at[SHARD + 1], halo_s.at[1], halo_r.at[1], (c + N_CTX - 1) % N_CTX, y))
    to_window = pltpu.make_async_copy(kv, kvw.at[pl.ds(1, SHARD)], loc.at[3])
    to_window.start()
    to_glob = pltpu.make_async_copy(kv.at[pl.ds(0, 2)], glob, loc.at[4])

    @pl.when(c == 0)
    def _():
        for j in range(1, NZ):
            remote(kv.at[pl.ds(0, 2)], glob, g_s.at[j - 1], g_r, at(0, j, 0), y).start()
        to_glob.start()

    for n, off in enumerate(offs):
        head = peer(off)
        go(remote(queries.at[:, pl.ds(pl.multiple_of(head * QCOL, QCOL), QCOL)],
                  qx.at[pl.ds(y * TOK, TOK)], q_s.at[n], q_r.at[n], c, head))

    def pick_to(source, buffer, base, lo, hi, dest_of):
        def body(n, _):
            dst = dest_of(n)
            slot = base + n - lo
            stage[slot] = buffer[table[dst * N_CTX + source]]
            remote(stage.at[slot], pool.at[source], st_s, pool_r, dst, y).start()
            return 0
        lax.fori_loop(lo, hi, body, 0)

    def plane(source, buffer, base):
        pool[source] = buffer[table[c * N_CTX + source]]
        pick_to(source, buffer, base, 1, 8, lambda n: at(n // 2, 0, n % 2))

    plane(c, kv, 0)

    below, above = at(0, NZ - 1, 0), at(0, 1, 0)
    for n, off in enumerate((0, *offs)):
        rows = pl.ds(peer(NY - off) * 4, 4)
        landed(before1.at[rows], m_s.at[0, n], m_r.at[0, n])
        go(remote(before1.at[rows], before2.at[rows], m_s.at[2, n], m_r.at[2, n], above, y))
        landed(after1.at[rows], m_s.at[1, n], m_r.at[1, n])
        go(remote(after1.at[rows], after2.at[rows], m_s.at[3, n], m_r.at[3, n], below, y))
    plane(below, before1, 7)
    plane(above, after1, 14)

    @pl.when(c == 0)
    def _():
        to_glob.wait()

    @pl.when(c != 0)
    def _():
        landed(glob, g_s.at[0], g_r)

    on_line = jnp.logical_and(x == 0, k == 0)

    @pl.when(on_line)
    def _():
        for j in range(1, 8):
            remote(glob, glob, g_s.at[6 + j], g_r, at(j // 2, 0, j % 2), y).start()

    to_window.wait()
    landed(kvw.at[0], halo_s.at[0], halo_r.at[0])
    landed(kvw.at[SHARD + 1], halo_s.at[1], halo_r.at[1])
    own_q.wait()
    for n, off in enumerate(offs):
        landed(qx.at[pl.ds(peer(NY - off) * TOK, TOK)], q_s.at[n], q_r.at[n])

    half = GROUP // 2

    def stacked(i, part):
        rows = pl.ds(i * BLOCK, BLOCK)
        return jnp.concatenate(
            [qx[rows, g * HEAD:(g + 1) * HEAD] for g in range(part * half, (part + 1) * half)], axis=0
        )

    def near(i, _):
        keys = jnp.concatenate(
            [kvw[pl.ds(i, 3), :, 0:HEAD].reshape(3 * BLOCK, HEAD),
             glob[:, :, 0:HEAD].reshape(2 * BLOCK, HEAD)], axis=0)
        values = jnp.concatenate(
            [kvw[pl.ds(i, 3), :, HEAD:ROW].reshape(3 * BLOCK, HEAD),
             glob[:, :, HEAD:ROW].reshape(2 * BLOCK, HEAD)], axis=0)
        for part in range(2):
            rows = slice(part * half * BLOCK, (part + 1) * half * BLOCK)
            scores = lax.dot_general(stacked(i, part), keys, NT, preferred_element_type=jnp.float32)
            largest = jnp.max(scores, axis=-1, keepdims=True)
            weights = jnp.exp2((scores - largest) * EXP2_SCALE)
            top[i, rows] = largest
            total[i, rows] = jnp.sum(weights, axis=-1, keepdims=True)
            acc[i, rows] = jnp.dot(weights.astype(jnp.bfloat16), values,
                                   preferred_element_type=jnp.float32)
        return 0

    lax.fori_loop(0, 8, near, 0)

    for n, off in enumerate((0, *offs)):
        rows = pl.ds(peer(NY - off) * 4, 4)
        landed(before2.at[rows], m_s.at[2, n], m_r.at[2, n])
        landed(after2.at[rows], m_s.at[3, n], m_r.at[3, n])
    below2, above2 = at(0, NZ - 2, 0), at(0, 2, 0)
    pick_to(below2, before2, 21, 0, 4, lambda n: at(n, 2, 0))
    pick_to(above2, after2, 25, 0, 4, lambda n: at(n, NZ - 2, 1))
    pick_to(below2, before2, 29, 0, 8, lambda n: at(n // 2, 1, n % 2))
    pick_to(above2, after2, 37, 0, 8, lambda n: at(n // 2, NZ - 1, n % 2))
    plane(below2, before2, 45)
    plane(above2, after2, 52)

    lax.fori_loop(8, 16, near, 0)

    landed(pool.at[pl.ds(0, SLOTS)], st_s, pool_r)

    def out_copy(j, i):
        column = pl.ds(pl.multiple_of(y * QCOL, QCOL), QCOL)
        return remote(outbox.at[pl.ds(i * BLOCK, BLOCK)],
                      out.at[pl.ds((i % 4) * BLOCK, BLOCK), column],
                      out_s.at[j], out_r.at[j], c, i // 4)

    def out_local(j, i):
        column = pl.ds(pl.multiple_of(y * QCOL, QCOL), QCOL)
        return pltpu.make_async_copy(outbox.at[pl.ds(i * BLOCK, BLOCK)],
                                     out.at[pl.ds((i % 4) * BLOCK, BLOCK), column], out_s.at[j])

    def block_of(j):
        step = j // 4
        off = jnp.where(step < 2, 2 - step, (3 - step) * 3)
        return ((y + off) % NY) * 4 + j % 4

    def finish(j, _):
        i = block_of(j)
        entry = (c * SHARD + i) * RAND
        chosen = [pool[rand[entry + r] // SHARD] for r in range(RAND)]
        keys = jnp.concatenate([b[:, 0:HEAD] for b in chosen], axis=0)
        values = jnp.concatenate([b[:, HEAD:ROW] for b in chosen], axis=0)
        for part in range(2):
            rows = slice(part * half * BLOCK, (part + 1) * half * BLOCK)
            scores = lax.dot_general(stacked(i, part), keys, NT, preferred_element_type=jnp.float32)
            early = top[i, rows]
            largest = jnp.maximum(early, jnp.max(scores, axis=-1, keepdims=True))
            weights = jnp.exp2((scores - largest) * EXP2_SCALE)
            fade = jnp.exp2((early - largest) * EXP2_SCALE)
            mass = total[i, rows] * fade + jnp.sum(weights, axis=-1, keepdims=True)
            mixed = acc[i, rows] * fade + jnp.dot(weights.astype(jnp.bfloat16), values,
                                                  preferred_element_type=jnp.float32)
            result = (mixed / mass).astype(jnp.bfloat16)
            for g in range(half):
                column = (part * half + g) * HEAD
                outbox[pl.ds(i * BLOCK, BLOCK), column:column + HEAD] = result[g * BLOCK:(g + 1) * BLOCK]

        @pl.when(j < 12)
        def _():
            out_copy(j, i).start()

        @pl.when(j >= 12)
        def _():
            out_local(j, i).start()
        return 0

    lax.fori_loop(0, 16, finish, 0)

    for copy in sends:
        copy.wait_send()

    @pl.when(c == 0)
    def _():
        for j in range(1, NZ):
            remote(kv.at[pl.ds(0, 2)], glob, g_s.at[j - 1], g_r, at(0, j, 0), y).wait_send()

    @pl.when(on_line)
    def _():
        for j in range(1, 8):
            remote(glob, glob, g_s.at[6 + j], g_r, at(j // 2, 0, j % 2), y).wait_send()

    everything = stage.at[pl.ds(0, SLOTS)]
    remote(everything, pool.at[pl.ds(0, SLOTS)], st_s, pool_r, at(0, 0, 1), y).wait_send()

    def drain(j, _):
        i = block_of(j)

        @pl.when(j < 12)
        def _():
            out_copy(j, i).wait()

        @pl.when(j >= 12)
        def _():
            out_local(j, i).wait()
        return 0

    lax.fori_loop(0, 16, drain, 0)


def shards(acts, queries, kv_weight, rand_blocks):
    flat_weight = kv_weight.reshape(MODEL, ROW)
    requests = rand_blocks.reshape(N_CTX, SHARD * RAND)
    holder = jnp.arange(N_CTX, dtype=jnp.int32)
    named = (requests // SHARD)[:, :, None] == holder[None, None, :]
    table = jnp.sum(jnp.where(named, (requests % SHARD)[:, :, None], 0), axis=1).astype(jnp.int32)
    bf16, f32 = jnp.bfloat16, jnp.float32
    blocks = pltpu.VMEM((SHARD, BLOCK, ROW), bf16)
    dma = pltpu.SemaphoreType.DMA
    return pl.pallas_call(
        kernel,
        out_shape=jax.ShapeDtypeStruct((TOK, NY * QCOL), bf16),
        in_specs=[pl.BlockSpec(memory_space=pltpu.SMEM)] * 2 + [pl.BlockSpec(memory_space=pl.ANY)] * 3,
        out_specs=pl.BlockSpec(memory_space=pl.ANY),
        scratch_shapes=[
            pltpu.VMEM((TOK, MODEL), bf16),
            pltpu.VMEM((NY, MODEL, ROW), bf16),
            pltpu.VMEM((3, 4, BLOCK, ROW), bf16),
            blocks,
            pltpu.VMEM((SHARD + 2, BLOCK, ROW), bf16),
            pltpu.VMEM((2, BLOCK, ROW), bf16),
            blocks, blocks, blocks, blocks,
            pltpu.VMEM((SLOTS, BLOCK, ROW), bf16),
            pltpu.VMEM((N_CTX, BLOCK, ROW), bf16),
            pltpu.VMEM((NY * TOK, QCOL), bf16),
            pltpu.VMEM((SHARD, GROUP * BLOCK, HEAD), f32),
            pltpu.VMEM((SHARD, GROUP * BLOCK, 1), f32),
            pltpu.VMEM((SHARD, GROUP * BLOCK, 1), f32),
            pltpu.VMEM((NY * TOK, QCOL), bf16),
            dma((5,)), dma((4,)), dma((4,)), dma((2, 3)), dma((2, 3)), dma((3, 4)), dma((3, 4)),
            dma((3,)), dma((3,)), dma((3,)), dma((3,)),
            dma((4, 4)), dma((4, 4)), dma, dma, dma((2,)), dma((2,)), dma((14,)), dma,
            dma((16,)), dma((16,)),
        ],
        compiler_params=pltpu.CompilerParams(
            has_side_effects=True, vmem_limit_bytes=60 * 1024 * 1024
        ),
        cost_estimate=pl.CostEstimate(
            flops=9 * 10**9, bytes_accessed=12 * 2**20, transcendentals=8 * 2**20
        ),
    )(table.reshape(-1), rand_blocks.reshape(-1), acts, queries, flat_weight)


def solution(mesh):
    placed = (P(("ctx", "fsdp"), None), P(("ctx", "fsdp"), None), P(None, "fsdp", None, None), P())
    return jax.shard_map(
        shards, mesh=mesh, in_specs=placed, out_specs=P(("ctx", "fsdp"), None), check_vma=False
    )
```

time: 610 us -> 166 us (0.27)
  waiting for transfers between devices: 320 us -> 0 us
  Pallas kernels: 0 us -> 156 us
  local copies, waits for them, and re-layouts: 161 us -> 9.07 us
  matrix products: 43.1 us -> 0 us
  blocking collectives: 30.7 us -> 0 us
  other arithmetic: 20.1 us -> 1.17 us
  starting transfers between devices: 18.9 us -> 0 us
  between operations: 13.6 us -> 0.03 us
    all_gather x1 -> x0, waiting for transfers between devices: 160 us -> none  [shards(): lax.all_gather(acts, 'fsdp', axis=0, tiled=True)]
    pallas_call x0 -> x1, Pallas kernels: none -> 156 us  [shards(): pl.pallas_call(kernel, out_shape=jax.ShapeDtypeStruct((TOK, NY * QCOL), b...]
    ppermute x2 -> x0, waiting for transfers between devices: 88.2 us -> none  [the longest x1 85.2 us: with_halo(): before = lax.ppermute(last, axis, up)]
    psum x1 -> x0, waiting for transfers between devices: 68.8 us -> none  [broadcast(): return lax.psum(block, axis)]
    gather x9 -> x0, local copies, waits for them, and re-layouts: 49 us -> none  [the longest x8 43.8 us: attend_group(): pool[id_part.reshape(-1)]]
    dot_general x17 -> x0, matrix products: 43.1 us -> none  [the longest x8 25.3 us: attend_group(): jnp.einsum('bhgqk,bkhd->bqhgd', probs, value_part, preferred_element_type...]
    unnamed x10 -> x3, local copies, waits for them, and re-layouts: 38.6 us -> 7.27 us
    all_to_all x1 -> x0, blocking collectives: 30.7 us -> none  [shards(): lax.all_to_all(attended, 'fsdp', split_axis=0, concat_axis=1, tiled=True)]
  transfers between devices with their start and end apart: 6 -> 0, of which waited for: 5 -> 0; matrix products, arithmetic and copies ran while one was open for 12% -> 0% of each run, Pallas kernels for 0% -> 0%
where the time goes in v1:
time: 166 us
  Pallas kernels  156 us (94%)
  local copies, waits for them, and re-layouts  9.07 us (5%)
    pallas_call x1, Pallas kernels, shards(): pl.pallas_call(kernel, out_shape=jax.ShapeDtypeStruct((TOK, NY * QCOL), b...  156 us
    unnamed x3, local copies, waits for them, and re-layouts  7.27 us

profile of v1, /device:TPU:1, one launch (start us, length us, event | category | flops | bytes accessed | tf_op | source)
XLA Modules:
  0.0 165.8 jit_solution(7686308046555969547)
XLA Ops:
  0.0 0.9 copy.7
  0.9 0.9 reshape.63.rand
  1.8 0.2 reshape.61
  2.1 1.1 select_reduce_fusion
  3.2 0.7 reshape.62.table
  3.9 3.2 %copy.11 = bf16[512,8,2,128]{3,1,2,0:T(8,128)(2,1)} copy(bf16[512,8,2,128]{3,2,1,0:T(2,128)(2,1)} %bitcast.5) | data formatting | bytes 4194304
  7.1 155.6 %shard_map.46 = bf16[512,2048]{1,0:T(8,128)(2,1)} custom-call(s32[4096]{0:T(1024)} %reshape.62.table, s32[3072]{0:T(1024)} %reshape.63.rand, bf16[512,4096]{1,0:T(8,128)(2,1)} %acts.1, bf16[512,2048]{1,0:T(8,128)(2,1)} %queries.1, bf16[4096,256]{1,0:T(8,128)(2,1)} %bitcast.6), custom_call_target="tpu_custom_call" | custom-call | flops 8999999488 | bytes 12582912 | tf_op jit(solution)/shard_map/pallas_call | solution.py:338
  162.7 3.2 %copy.13 = bf16[512,2048]{1,0:T(8,128)(2,1)} copy(bf16[512,2048]{1,0:T(8,128)(2,1)} %shard_map.46) | data formatting | bytes 4194304
  (1 shorter events, 0.0 us)

commit v2 on v1

--- a/solution.py
+++ b/solution.py
@@ -26,9 +26,9 @@
 
 
 def kernel(
-    table, rand, acts, queries, weight, out,
+    rand, acts, queries, weight, out,
     acts_v, wbuf, kv_send, kv, kvw, glob, before1, after1, before2, after2,
-    stage, pool, qx, acc, top, total, outbox,
+    stage, pool, qx, acc, top, total, outbox, table, pairs,
     loc, wy_s, wy_r, wd_s, wd_r, wx_s, wx_r, kv_s, kv_r, q_s, q_r,
     m_s, m_r, st_s, pool_r, halo_s, halo_r, g_s, g_r, out_s, out_r,
 ):
@@ -62,19 +62,46 @@
     whole = pl.ds(mine, QUARTER)
     first = pl.ds(mine, QUARTER // 2)
     second = pl.ds(mine + QUARTER // 2, QUARTER // 2)
-    for n, off in enumerate((1, 3)):
-        go(remote(weight.at[whole], wbuf.at[y, whole], wy_s.at[n], wy_r.at[n], c, peer(off)))
-    acts_in = pltpu.make_async_copy(acts, acts_v, loc.at[0])
-    acts_in.start()
-    own_w = pltpu.make_async_copy(weight, wbuf.at[y], loc.at[1])
+    barrier = pltpu.get_barrier_semaphore()
+
+    def greet(ctx, head):
+        pl.semaphore_signal(barrier, inc=1, device_id=(ctx, head), device_id_type=pl.DeviceIdType.MESH)
+
+    for off in range(1, NY):
+        greet(c, peer(off))
+    for dz in (1, NZ - 1, 2, NZ - 2):
+        greet(at(0, dz, 0), y)
+    for n in range(1, 8):
+        greet(at(n // 2, 0, n % 2), y)
+    own_w = pltpu.make_async_copy(weight, pairs, loc.at[1])
     own_w.start()
     own_q = pltpu.make_async_copy(
         queries.at[:, pl.ds(pl.multiple_of(y * QCOL, QCOL), QCOL)],
         qx.at[pl.ds(y * TOK, TOK)], loc.at[2],
     )
+    acts_in = pltpu.make_async_copy(acts, acts_v, loc.at[0])
+    acts_in.start()
     own_q.start()
+    own_w.wait()
+
+    line = lax.broadcasted_iota(jnp.int32, (2 * BLOCK, 2 * BLOCK), 0)
+    place = lax.broadcasted_iota(jnp.int32, (2 * BLOCK, 2 * BLOCK), 1)
+    wanted = jnp.where(line < BLOCK, 2 * line, 2 * (line - BLOCK) + 1)
+    order = jnp.where(place == wanted, 1.0, 0.0).astype(jnp.bfloat16)
+
+    def set_apart(b, _):
+        parts = jnp.dot(order, pairs[pl.ds(b * ROW, ROW)], preferred_element_type=jnp.float32)
+        parts = parts.astype(jnp.bfloat16)
+        rows = pl.ds(b * BLOCK, BLOCK)
+        wbuf[y, rows, 0:HEAD] = parts[0:BLOCK]
+        wbuf[y, rows, HEAD:ROW] = parts[BLOCK:2 * BLOCK]
+        return 0
+
+    lax.fori_loop(0, MODEL // BLOCK, set_apart, 0, unroll=4)
+    pl.semaphore_wait(barrier, 14)
+    for n, off in enumerate((1, 3)):
+        go(remote(wbuf.at[y, whole], wbuf.at[y, whole], wy_s.at[n], wy_r.at[n], c, peer(off)))
     acts_in.wait()
-    own_w.wait()
 
     def project(head, dest, lead):
         def tile(t, _):
@@ -91,6 +118,69 @@
 
     project(y, kv, y * 4)
 
+    offs = (1, 3, 2)
+
+    def landed(view, send, recv):
+        remote(view, view, send, recv, at(0, 0, 1), y).wait_recv()
+
+    below, above = at(0, NZ - 1, 0), at(0, 1, 0)
+    below2, above2 = at(0, NZ - 2, 0), at(0, 2, 0)
+
+    def in_plane(n):
+        return at(n // 2, 0, n % 2)
+
+    groups = {
+        "own": (c, 0, 1, 8, in_plane),
+        "below": (below, 7, 1, 8, in_plane),
+        "above": (above, 14, 1, 8, in_plane),
+        "below2 far": (below2, 21, 0, 4, lambda n: at(n, 2, 0)),
+        "above2 far": (above2, 25, 0, 4, lambda n: at(n, NZ - 2, 1)),
+        "below2 next": (below2, 29, 0, 8, lambda n: at(n // 2, 1, n % 2)),
+        "above2 next": (above2, 37, 0, 8, lambda n: at(n // 2, NZ - 1, n % 2)),
+        "below2": (below2, 45, 1, 8, in_plane),
+        "above2": (above2, 52, 1, 8, in_plane),
+    }
+    keep = {"own": 59, "below": 60, "above": 61, "below2": 62, "above2": 63}
+
+    def named_block(dst, source):
+        found = jnp.int32(0)
+        for r in range(RAND):
+            for b in range(SHARD):
+                v = rand[r * N_CTX * SHARD + dst * SHARD + b]
+                found += jnp.where(v >> 4 == source, v & 15, 0)
+        return found
+
+    def look_up(name):
+        source, base, lo, hi, dest_of = groups[name]
+
+        def body(n, _):
+            table[base + n - lo] = named_block(dest_of(n), source)
+            return 0
+
+        lax.fori_loop(lo, hi, body, 0)
+        if name in keep:
+            table[keep[name]] = named_block(c, source)
+
+    def pick(name, buffer):
+        source, base, lo, hi, dest_of = groups[name]
+        if name in keep:
+            pool[source] = buffer[table[keep[name]]]
+
+        def body(n, _):
+            slot = base + n - lo
+            stage[slot] = buffer[table[slot]]
+            remote(stage.at[slot], pool.at[source], st_s, pool_r, dest_of(n), y).start()
+            return 0
+
+        lax.fori_loop(lo, hi, body, 0)
+
+    def forward(n):
+        rows = pl.ds(peer(NY - (0, *offs)[n]) * 4, 4)
+        landed(before1.at[rows], m_s.at[0, n], m_r.at[0, n])
+        go(remote(before1.at[rows], before2.at[rows], m_s.at[2, n], m_r.at[2, n], above, y))
+        landed(after1.at[rows], m_s.at[1, n], m_r.at[1, n])
+        go(remote(after1.at[rows], after2.at[rows], m_s.at[3, n], m_r.at[3, n], below, y))
+
     def multicast(n, head):
         rows = pl.ds(head * 4, 4)
         go(remote(kv.at[rows], before1.at[rows], m_s.at[0, n], m_r.at[0, n], at(0, 1, 0), y))
@@ -105,8 +195,9 @@
             go(remote(wbuf.at[head, rows], wbuf.at[head, rows], wx_s.at[n, j], wx_r.at[n, j],
                       at(dx, dz, 0), y))
 
-    def landed(view, send, recv):
-        remote(view, view, send, recv, at(0, 0, 1), y).wait_recv()
+    multicast(0, y)
+    for name in groups:
+        look_up(name)
 
     landed(wbuf.at[peer(3), whole], wy_s.at[0], wy_r.at[0])
     go(remote(wbuf.at[peer(3), first], wbuf.at[peer(3), first], wy_s.at[2], wy_r.at[2], c, peer(1)))
@@ -114,12 +205,11 @@
     go(remote(wbuf.at[peer(1), second], wbuf.at[peer(1), second], wy_s.at[3], wy_r.at[3], c, peer(3)))
     spread(0, 1)
     spread(1, 3)
-    multicast(0, y)
+    forward(0)
     landed(wbuf.at[peer(2), first], wy_s.at[2], wy_r.at[2])
     landed(wbuf.at[peer(2), second], wy_s.at[3], wy_r.at[3])
     spread(2, 2)
 
-    offs = (1, 3, 2)
     far = pl.ds(other, QUARTER)
     sib_mine = pl.ds((parity * 2 + 1 - k) * QUARTER, QUARTER)
     sib_other = pl.ds(((1 - parity) * 2 + 1 - k) * QUARTER, QUARTER)
@@ -134,67 +224,76 @@
         project(head, kv_send.at[n], 0)
         go(remote(kv_send.at[n], kv.at[pl.ds(y * 4, 4)], kv_s.at[n], kv_r.at[n], c, head))
 
+    to_glob = pltpu.make_async_copy(kv.at[pl.ds(0, 2)], glob, loc.at[4])
+
+    def root_copies():
+        return [remote(kv.at[pl.ds(0, 2)], glob, g_s.at[n], g_r, at(0, dz, 0), y)
+                for n, dz in enumerate((2, NZ - 2, 1, NZ - 1))]
+
+    def up_copies():
+        return [remote(glob, glob, g_s.at[4 + n], g_r, at(0, dz, 0), y) for n, dz in enumerate((2, 1))]
+
+    def down_copies():
+        return [remote(glob, glob, g_s.at[6], g_r, at(0, NZ - 1, 0), y)]
+
+    def plane_copies():
+        return [remote(glob, glob, g_s.at[6 + j], g_r, at(j // 2, 0, j % 2), y) for j in range(1, 8)]
+
+    on_line = jnp.logical_and(x == 0, k == 0)
+    tree = (
+        (jnp.logical_and(on_line, z == 2), up_copies),
+        (jnp.logical_and(on_line, z == NZ - 2), down_copies),
+        (on_line, plane_copies),
+    )
+
+    def send_globals(holder):
+        @pl.when(jnp.logical_and(c == 0, holder == 0))
+        def _():
+            for copy in root_copies():
+                copy.start()
+            to_glob.start()
+
+    send_globals(y)
+
     for n, off in enumerate(offs):
         head = peer(NY - off)
         landed(kv.at[pl.ds(head * 4, 4)], kv_s.at[n], kv_r.at[n])
+        send_globals(head)
         multicast(n + 1, head)
+        if n:
+            forward(n)
+
+    @pl.when(c == 0)
+    def _():
+        to_glob.wait()
+
+    @pl.when(jnp.logical_and(on_line, c != 0))
+    def _():
+        landed(glob, g_s.at[0], g_r)
+
+    for holds, copies in tree:
+        @pl.when(holds)
+        def _():
+            for copy in copies():
+                copy.start()
 
     go(remote(kv.at[SHARD - 1], kvw.at[0], halo_s.at[0], halo_r.at[0], (c + 1) % N_CTX, y))
     go(remote(kv.at[0], kvw.at[SHARD + 1], halo_s.at[1], halo_r.at[1], (c + N_CTX - 1) % N_CTX, y))
     to_window = pltpu.make_async_copy(kv, kvw.at[pl.ds(1, SHARD)], loc.at[3])
     to_window.start()
-    to_glob = pltpu.make_async_copy(kv.at[pl.ds(0, 2)], glob, loc.at[4])
-
-    @pl.when(c == 0)
-    def _():
-        for j in range(1, NZ):
-            remote(kv.at[pl.ds(0, 2)], glob, g_s.at[j - 1], g_r, at(0, j, 0), y).start()
-        to_glob.start()
-
     for n, off in enumerate(offs):
         head = peer(off)
         go(remote(queries.at[:, pl.ds(pl.multiple_of(head * QCOL, QCOL), QCOL)],
                   qx.at[pl.ds(y * TOK, TOK)], q_s.at[n], q_r.at[n], c, head))
 
-    def pick_to(source, buffer, base, lo, hi, dest_of):
-        def body(n, _):
-            dst = dest_of(n)
-            slot = base + n - lo
-            stage[slot] = buffer[table[dst * N_CTX + source]]
-            remote(stage.at[slot], pool.at[source], st_s, pool_r, dst, y).start()
-            return 0
-        lax.fori_loop(lo, hi, body, 0)
-
-    def plane(source, buffer, base):
-        pool[source] = buffer[table[c * N_CTX + source]]
-        pick_to(source, buffer, base, 1, 8, lambda n: at(n // 2, 0, n % 2))
-
-    plane(c, kv, 0)
-
-    below, above = at(0, NZ - 1, 0), at(0, 1, 0)
-    for n, off in enumerate((0, *offs)):
-        rows = pl.ds(peer(NY - off) * 4, 4)
-        landed(before1.at[rows], m_s.at[0, n], m_r.at[0, n])
-        go(remote(before1.at[rows], before2.at[rows], m_s.at[2, n], m_r.at[2, n], above, y))
-        landed(after1.at[rows], m_s.at[1, n], m_r.at[1, n])
-        go(remote(after1.at[rows], after2.at[rows], m_s.at[3, n], m_r.at[3, n], below, y))
-    plane(below, before1, 7)
-    plane(above, after1, 14)
-
-    @pl.when(c == 0)
-    def _():
-        to_glob.wait()
-
-    @pl.when(c != 0)
+    pick("own", kv)
+    forward(3)
+    pick("below", before1)
+    pick("above", after1)
+
+    @pl.when(jnp.logical_not(on_line))
     def _():
         landed(glob, g_s.at[0], g_r)
-
-    on_line = jnp.logical_and(x == 0, k == 0)
-
-    @pl.when(on_line)
-    def _():
-        for j in range(1, 8):
-            remote(glob, glob, g_s.at[6 + j], g_r, at(j // 2, 0, j % 2), y).start()
 
     to_window.wait()
     landed(kvw.at[0], halo_s.at[0], halo_r.at[0])
@@ -235,13 +334,12 @@
         rows = pl.ds(peer(NY - off) * 4, 4)
         landed(before2.at[rows], m_s.at[2, n], m_r.at[2, n])
         landed(after2.at[rows], m_s.at[3, n], m_r.at[3, n])
-    below2, above2 = at(0, NZ - 2, 0), at(0, 2, 0)
-    pick_to(below2, before2, 21, 0, 4, lambda n: at(n, 2, 0))
-    pick_to(above2, after2, 25, 0, 4, lambda n: at(n, NZ - 2, 1))
-    pick_to(below2, before2, 29, 0, 8, lambda n: at(n // 2, 1, n % 2))
-    pick_to(above2, after2, 37, 0, 8, lambda n: at(n // 2, NZ - 1, n % 2))
-    plane(below2, before2, 45)
-    plane(above2, after2, 52)
+    pick("below2 far", before2)
+    pick("above2 far", after2)
+    pick("below2 next", before2)
+    pick("above2 next", after2)
+    pick("below2", before2)
+    pick("above2", after2)
 
     lax.fori_loop(8, 16, near, 0)
 
@@ -265,8 +363,7 @@
 
     def finish(j, _):
         i = block_of(j)
-        entry = (c * SHARD + i) * RAND
-        chosen = [pool[rand[entry + r] // SHARD] for r in range(RAND)]
+        chosen = [pool[rand[r * N_CTX * SHARD + c * SHARD + i] >> 4] for r in range(RAND)]
         keys = jnp.concatenate([b[:, 0:HEAD] for b in chosen], axis=0)
         values = jnp.concatenate([b[:, HEAD:ROW] for b in chosen], axis=0)
         for part in range(2):
@@ -298,15 +395,11 @@
     for copy in sends:
         copy.wait_send()
 
-    @pl.when(c == 0)
-    def _():
-        for j in range(1, NZ):
-            remote(kv.at[pl.ds(0, 2)], glob, g_s.at[j - 1], g_r, at(0, j, 0), y).wait_send()
-
-    @pl.when(on_line)
-    def _():
-        for j in range(1, 8):
-            remote(glob, glob, g_s.at[6 + j], g_r, at(j // 2, 0, j % 2), y).wait_send()
+    for holds, copies in ((c == 0, root_copies), *tree):
+        @pl.when(holds)
+        def _():
+            for copy in copies():
+                copy.wait_send()
 
     everything = stage.at[pl.ds(0, SLOTS)]
     remote(everything, pool.at[pl.ds(0, SLOTS)], st_s, pool_r, at(0, 0, 1), y).wait_send()
@@ -327,18 +420,14 @@
 
 
 def shards(acts, queries, kv_weight, rand_blocks):
-    flat_weight = kv_weight.reshape(MODEL, ROW)
-    requests = rand_blocks.reshape(N_CTX, SHARD * RAND)
-    holder = jnp.arange(N_CTX, dtype=jnp.int32)
-    named = (requests // SHARD)[:, :, None] == holder[None, None, :]
-    table = jnp.sum(jnp.where(named, (requests % SHARD)[:, :, None], 0), axis=1).astype(jnp.int32)
+    flat_weight = kv_weight.reshape(2 * MODEL, HEAD)
     bf16, f32 = jnp.bfloat16, jnp.float32
     blocks = pltpu.VMEM((SHARD, BLOCK, ROW), bf16)
     dma = pltpu.SemaphoreType.DMA
     return pl.pallas_call(
         kernel,
         out_shape=jax.ShapeDtypeStruct((TOK, NY * QCOL), bf16),
-        in_specs=[pl.BlockSpec(memory_space=pltpu.SMEM)] * 2 + [pl.BlockSpec(memory_space=pl.ANY)] * 3,
+        in_specs=[pl.BlockSpec(memory_space=pltpu.SMEM)] + [pl.BlockSpec(memory_space=pl.ANY)] * 3,
         out_specs=pl.BlockSpec(memory_space=pl.ANY),
         scratch_shapes=[
             pltpu.VMEM((TOK, MODEL), bf16),
@@ -355,18 +444,20 @@
             pltpu.VMEM((SHARD, GROUP * BLOCK, 1), f32),
             pltpu.VMEM((SHARD, GROUP * BLOCK, 1), f32),
             pltpu.VMEM((NY * TOK, QCOL), bf16),
+            pltpu.SMEM((N_CTX,), jnp.int32),
+            pltpu.VMEM((2 * MODEL, HEAD), bf16),
             dma((5,)), dma((4,)), dma((4,)), dma((2, 3)), dma((2, 3)), dma((3, 4)), dma((3, 4)),
             dma((3,)), dma((3,)), dma((3,)), dma((3,)),
             dma((4, 4)), dma((4, 4)), dma, dma, dma((2,)), dma((2,)), dma((14,)), dma,
             dma((16,)), dma((16,)),
         ],
         compiler_params=pltpu.CompilerParams(
-            has_side_effects=True, vmem_limit_bytes=60 * 1024 * 1024
+            collective_id=0, has_side_effects=True, vmem_limit_bytes=60 * 1024 * 1024
         ),
         cost_estimate=pl.CostEstimate(
             flops=9 * 10**9, bytes_accessed=12 * 2**20, transcendentals=8 * 2**20
         ),
-    )(table.reshape(-1), rand_blocks.reshape(-1), acts, queries, flat_weight)
+    )(rand_blocks.T.reshape(-1), acts, queries, flat_weight)
 
 
 def solution(mesh):

time: 166 us -> 154 us (0.928)
  Pallas kernels: 156 us -> 149 us
  local copies, waits for them, and re-layouts: 9.07 us -> 4.48 us
    pallas_call x1, Pallas kernels: 156 us -> 149 us  [shards(): pl.pallas_call(kernel, out_shape=jax.ShapeDtypeStruct((TOK, NY * QCOL), b...]
    unnamed x3 -> x1, local copies, waits for them, and re-layouts: 7.27 us -> 3.16 us
where the time goes in v2:
time: 154 us
  Pallas kernels  149 us (97%)
  local copies, waits for them, and re-layouts  4.48 us (3%)
    pallas_call x1, Pallas kernels, shards(): pl.pallas_call(kernel, out_shape=jax.ShapeDtypeStruct((TOK, NY * QCOL), b...  149 us
    unnamed x1, local copies, waits for them, and re-layouts  3.16 us

profile of v2, /device:TPU:1, one launch (start us, length us, event | category | flops | bytes accessed | tf_op | source)
XLA Modules:
  0.0 154.0 jit_solution(11810168420416409196)
XLA Ops:
  0.0 1.3 reshape.6.rand
  1.3 149.5 %shard_map.46 = bf16[512,2048]{1,0:T(8,128)(2,1)} custom-call(s32[3072]{0:T(1024)} %reshape.6.rand, bf16[512,4096]{1,0:T(8,128)(2,1)} %acts.1, bf16[512,2048]{1,0:T(8,128)(2,1)} %queries.1, bf16[8192,128]{1,0:T(8,128)(2,1)} %bitcast.3), custom_call_target="tpu_custom_call" | custom-call | flops 8999999488 | bytes 12582912 | tf_op jit(solution)/shard_map/pallas_call | solution.py:427
  150.8 3.2 %copy.6 = bf16[512,2048]{1,0:T(8,128)(2,1)} copy(bf16[512,2048]{1,0:T(8,128)(2,1)} %shard_map.46) | data formatting | bytes 4194304

commit v3 on v2

--- a/solution.py
+++ b/solution.py
@@ -20,17 +20,17 @@
 QCOL = GROUP * HEAD
 QUARTER = MODEL // 4
 SUB = QUARTER // 4
-SLOTS = 59
+SLOTS = 61
 EXP2_SCALE = math.log2(math.e) / math.sqrt(HEAD)
 NT = (((1,), (1,)), ((), ()))
 
 
 def kernel(
     rand, acts, queries, weight, out,
-    acts_v, wbuf, kv_send, kv, kvw, glob, before1, after1, before2, after2,
+    acts_v, wbuf, kv_send, kv, kvw, glob, before, after,
     stage, pool, qx, acc, top, total, outbox, table, pairs,
     loc, wy_s, wy_r, wd_s, wd_r, wx_s, wx_r, kv_s, kv_r, q_s, q_r,
-    m_s, m_r, st_s, pool_r, halo_s, halo_r, g_s, g_r, out_s, out_r,
+    m_s, m_r, st_s, pool_r, halo_s, halo_r, g_s, g_r, out_s, out_r, near_by,
 ):
     c = lax.axis_index("ctx")
     y = lax.axis_index("fsdp")
@@ -69,7 +69,8 @@
 
     for off in range(1, NY):
         greet(c, peer(off))
-    for dz in (1, NZ - 1, 2, NZ - 2):
+    along = (1, NZ - 1, 2, NZ - 2, 3, NZ - 3)
+    for dz in along:
         greet(at(0, dz, 0), y)
     for n in range(1, 8):
         greet(at(n // 2, 0, n % 2), y)
@@ -98,9 +99,11 @@
         return 0
 
     lax.fori_loop(0, MODEL // BLOCK, set_apart, 0, unroll=4)
-    pl.semaphore_wait(barrier, 14)
-    for n, off in enumerate((1, 3)):
-        go(remote(wbuf.at[y, whole], wbuf.at[y, whole], wy_s.at[n], wy_r.at[n], c, peer(off)))
+    pl.semaphore_wait(barrier, 16)
+    for n, (off, rows) in enumerate(((1, first), (3, second), (1, second), (3, first))):
+        go(remote(wbuf.at[y, rows], wbuf.at[y, rows], wy_s.at[n], wy_r.at[n], c, peer(off)))
+    for dz in along:
+        pl.semaphore_signal(near_by, inc=1, device_id=(at(0, dz, 0), y), device_id_type=pl.DeviceIdType.MESH)
     acts_in.wait()
 
     def project(head, dest, lead):
@@ -124,23 +127,22 @@
         remote(view, view, send, recv, at(0, 0, 1), y).wait_recv()
 
     below, above = at(0, NZ - 1, 0), at(0, 1, 0)
-    below2, above2 = at(0, NZ - 2, 0), at(0, 2, 0)
 
     def in_plane(n):
         return at(n // 2, 0, n % 2)
 
     groups = {
         "own": (c, 0, 1, 8, in_plane),
-        "below": (below, 7, 1, 8, in_plane),
-        "above": (above, 14, 1, 8, in_plane),
-        "below2 far": (below2, 21, 0, 4, lambda n: at(n, 2, 0)),
-        "above2 far": (above2, 25, 0, 4, lambda n: at(n, NZ - 2, 1)),
-        "below2 next": (below2, 29, 0, 8, lambda n: at(n // 2, 1, n % 2)),
-        "above2 next": (above2, 37, 0, 8, lambda n: at(n // 2, NZ - 1, n % 2)),
-        "below2": (below2, 45, 1, 8, in_plane),
-        "above2": (above2, 52, 1, 8, in_plane),
+        "below 3": (below, 7, 0, 4, lambda n: at(n, 3, 0)),
+        "above 3": (above, 11, 0, 4, lambda n: at(n, NZ - 3, 1)),
+        "below 2": (below, 15, 0, 8, lambda n: at(n // 2, 2, n % 2)),
+        "above 2": (above, 23, 0, 8, lambda n: at(n // 2, NZ - 2, n % 2)),
+        "below 1": (below, 31, 0, 8, lambda n: at(n // 2, 1, n % 2)),
+        "above 1": (above, 39, 0, 8, lambda n: at(n // 2, NZ - 1, n % 2)),
+        "below": (below, 47, 1, 8, in_plane),
+        "above": (above, 54, 1, 8, in_plane),
     }
-    keep = {"own": 59, "below": 60, "above": 61, "below2": 62, "above2": 63}
+    keep = {"own": 61, "below": 62, "above": 63}
 
     def named_block(dst, source):
         found = jnp.int32(0)
@@ -174,23 +176,21 @@
 
         lax.fori_loop(lo, hi, body, 0)
 
-    def forward(n):
-        rows = pl.ds(peer(NY - (0, *offs)[n]) * 4, 4)
-        landed(before1.at[rows], m_s.at[0, n], m_r.at[0, n])
-        go(remote(before1.at[rows], before2.at[rows], m_s.at[2, n], m_r.at[2, n], above, y))
-        landed(after1.at[rows], m_s.at[1, n], m_r.at[1, n])
-        go(remote(after1.at[rows], after2.at[rows], m_s.at[3, n], m_r.at[3, n], below, y))
-
     def multicast(n, head):
         rows = pl.ds(head * 4, 4)
-        go(remote(kv.at[rows], before1.at[rows], m_s.at[0, n], m_r.at[0, n], at(0, 1, 0), y))
-        go(remote(kv.at[rows], after1.at[rows], m_s.at[1, n], m_r.at[1, n], at(0, -1 + NZ, 0), y))
-
-    def spread(n, off):
+        go(remote(kv.at[rows], before.at[rows], m_s.at[0, n], m_r.at[0, n], at(0, 1, 0), y))
+        go(remote(kv.at[rows], after.at[rows], m_s.at[1, n], m_r.at[1, n], at(0, -1 + NZ, 0), y))
+
+    def to_sibling(n, off):
         head = peer(off)
         go(remote(wbuf.at[head, whole], wbuf.at[head, whole], wd_s.at[0, n], wd_r.at[0, n],
                   at(0, 0, 1), y))
-        for j, (dx, dz) in enumerate(((1, 0), (NX - 1, 0), (0, 1), (0, NZ - 1))):
+
+    def to_chips(n, off, part):
+        head = peer(off)
+        steps = ((1, 0), (NX - 1, 0), (0, 1), (0, NZ - 1))
+        for j in (2 * part, 2 * part + 1):
+            dx, dz = steps[j]
             rows = pl.ds(mine + j * SUB, SUB)
             go(remote(wbuf.at[head, rows], wbuf.at[head, rows], wx_s.at[n, j], wx_r.at[n, j],
                       at(dx, dz, 0), y))
@@ -199,30 +199,48 @@
     for name in groups:
         look_up(name)
 
-    landed(wbuf.at[peer(3), whole], wy_s.at[0], wy_r.at[0])
-    go(remote(wbuf.at[peer(3), first], wbuf.at[peer(3), first], wy_s.at[2], wy_r.at[2], c, peer(1)))
-    landed(wbuf.at[peer(1), whole], wy_s.at[1], wy_r.at[1])
-    go(remote(wbuf.at[peer(1), second], wbuf.at[peer(1), second], wy_s.at[3], wy_r.at[3], c, peer(3)))
-    spread(0, 1)
-    spread(1, 3)
-    forward(0)
-    landed(wbuf.at[peer(2), first], wy_s.at[2], wy_r.at[2])
-    landed(wbuf.at[peer(2), second], wy_s.at[3], wy_r.at[3])
-    spread(2, 2)
+    landed(wbuf.at[peer(3), first], wy_s.at[0], wy_r.at[0])
+    go(remote(wbuf.at[peer(3), first], wbuf.at[peer(3), first], wy_s.at[4], wy_r.at[4], c, peer(1)))
+    to_chips(1, 3, 0)
+    landed(wbuf.at[peer(1), second], wy_s.at[1], wy_r.at[1])
+    go(remote(wbuf.at[peer(1), second], wbuf.at[peer(1), second], wy_s.at[5], wy_r.at[5], c, peer(3)))
+    to_chips(0, 1, 1)
+    landed(wbuf.at[peer(3), second], wy_s.at[2], wy_r.at[2])
+    to_chips(1, 3, 1)
+    to_sibling(1, 3)
+    landed(wbuf.at[peer(1), first], wy_s.at[3], wy_r.at[3])
+    to_chips(0, 1, 0)
+    to_sibling(0, 1)
 
     far = pl.ds(other, QUARTER)
     sib_mine = pl.ds((parity * 2 + 1 - k) * QUARTER, QUARTER)
     sib_other = pl.ds(((1 - parity) * 2 + 1 - k) * QUARTER, QUARTER)
-    for n, off in enumerate(offs):
+
+    def pass_far(n, off):
         head = peer(off)
         for j in range(4):
             landed(wbuf.at[head, pl.ds(other + j * SUB, SUB)], wx_s.at[n, j], wx_r.at[n, j])
         go(remote(wbuf.at[head, far], wbuf.at[head, far], wd_s.at[1, n], wd_r.at[1, n],
                   at(0, 0, 1), y))
+
+    def serve(n, off):
+        head = peer(off)
         landed(wbuf.at[head, sib_mine], wd_s.at[0, n], wd_r.at[0, n])
         landed(wbuf.at[head, sib_other], wd_s.at[1, n], wd_r.at[1, n])
         project(head, kv_send.at[n], 0)
         go(remote(kv_send.at[n], kv.at[pl.ds(y * 4, 4)], kv_s.at[n], kv_r.at[n], c, head))
+
+    pass_far(0, 1)
+    pass_far(1, 3)
+    landed(wbuf.at[peer(2), first], wy_s.at[4], wy_r.at[4])
+    to_chips(2, 2, 0)
+    landed(wbuf.at[peer(2), second], wy_s.at[5], wy_r.at[5])
+    to_chips(2, 2, 1)
+    to_sibling(2, 2)
+    serve(0, 1)
+    serve(1, 3)
+    pass_far(2, 2)
+    serve(2, 2)
 
     to_glob = pltpu.make_async_copy(kv.at[pl.ds(0, 2)], glob, loc.at[4])
 
@@ -260,8 +278,6 @@
         landed(kv.at[pl.ds(head * 4, 4)], kv_s.at[n], kv_r.at[n])
         send_globals(head)
         multicast(n + 1, head)
-        if n:
-            forward(n)
 
     @pl.when(c == 0)
     def _():
@@ -287,9 +303,14 @@
                   qx.at[pl.ds(y * TOK, TOK)], q_s.at[n], q_r.at[n], c, head))
 
     pick("own", kv)
-    forward(3)
-    pick("below", before1)
-    pick("above", after1)
+    for n, off in enumerate((0, *offs)):
+        rows = pl.ds(peer(NY - off) * 4, 4)
+        landed(before.at[rows], m_s.at[0, n], m_r.at[0, n])
+        landed(after.at[rows], m_s.at[1, n], m_r.at[1, n])
+    pl.semaphore_wait(near_by, len(along))
+    for name in groups:
+        if name != "own":
+            pick(name, before if name.startswith("below") else after)
 
     @pl.when(jnp.logical_not(on_line))
     def _():
@@ -328,20 +349,7 @@
                                    preferred_element_type=jnp.float32)
         return 0
 
-    lax.fori_loop(0, 8, near, 0)
-
-    for n, off in enumerate((0, *offs)):
-        rows = pl.ds(peer(NY - off) * 4, 4)
-        landed(before2.at[rows], m_s.at[2, n], m_r.at[2, n])
-        landed(after2.at[rows], m_s.at[3, n], m_r.at[3, n])
-    pick("below2 far", before2)
-    pick("above2 far", after2)
-    pick("below2 next", before2)
-    pick("above2 next", after2)
-    pick("below2", before2)
-    pick("above2", after2)
-
-    lax.fori_loop(8, 16, near, 0)
+    lax.fori_loop(0, SHARD, near, 0)
 
     landed(pool.at[pl.ds(0, SLOTS)], st_s, pool_r)
 
@@ -436,7 +444,7 @@
             blocks,
             pltpu.VMEM((SHARD + 2, BLOCK, ROW), bf16),
             pltpu.VMEM((2, BLOCK, ROW), bf16),
-            blocks, blocks, blocks, blocks,
+            blocks, blocks,
             pltpu.VMEM((SLOTS, BLOCK, ROW), bf16),
             pltpu.VMEM((N_CTX, BLOCK, ROW), bf16),
             pltpu.VMEM((NY * TOK, QCOL), bf16),
@@ -446,10 +454,10 @@
             pltpu.VMEM((NY * TOK, QCOL), bf16),
             pltpu.SMEM((N_CTX,), jnp.int32),
             pltpu.VMEM((2 * MODEL, HEAD), bf16),
-            dma((5,)), dma((4,)), dma((4,)), dma((2, 3)), dma((2, 3)), dma((3, 4)), dma((3, 4)),
+            dma((5,)), dma((6,)), dma((6,)), dma((2, 3)), dma((2, 3)), dma((3, 4)), dma((3, 4)),
             dma((3,)), dma((3,)), dma((3,)), dma((3,)),
-            dma((4, 4)), dma((4, 4)), dma, dma, dma((2,)), dma((2,)), dma((14,)), dma,
-            dma((16,)), dma((16,)),
+            dma((2, 4)), dma((2, 4)), dma, dma, dma((2,)), dma((2,)), dma((14,)), dma,
+            dma((16,)), dma((16,)), pltpu.SemaphoreType.REGULAR,
         ],
         compiler_params=pltpu.CompilerParams(
             collective_id=0, has_side_effects=True, vmem_limit_bytes=60 * 1024 * 1024

time: 154 us -> 151 us (0.981); the launches traced: 154 us -> 148 us
  Pallas kernels: 149 us -> 144 us
    pallas_call x1, Pallas kernels: 149 us -> 144 us  [shards(): pl.pallas_call(kernel, out_shape=jax.ShapeDtypeStruct((TOK, NY * QCOL), b...]
where the time goes in v3:
time: 151 us; the launch traced here: 148 us
  Pallas kernels  144 us (95%)
  local copies, waits for them, and re-layouts  4.48 us (3%)
    pallas_call x1, Pallas kernels, shards(): pl.pallas_call(kernel, out_shape=jax.ShapeDtypeStruct((TOK, NY * QCOL), b...  144 us
    unnamed x1, local copies, waits for them, and re-layouts  3.16 us

profile of v3, /device:TPU:1, one launch (start us, length us, event | category | flops | bytes accessed | tf_op | source)
XLA Modules:
  0.0 148.5 jit_solution(1982132090550158202)
XLA Ops:
  0.0 1.3 reshape.6.rand
  1.3 144.0 %shard_map.46 = bf16[512,2048]{1,0:T(8,128)(2,1)} custom-call(s32[3072]{0:T(1024)} %reshape.6.rand, bf16[512,4096]{1,0:T(8,128)(2,1)} %acts.1, bf16[512,2048]{1,0:T(8,128)(2,1)} %queries.1, bf16[8192,128]{1,0:T(8,128)(2,1)} %bitcast.3), custom_call_target="tpu_custom_call" | custom-call | flops 8999999488 | bytes 12582912 | tf_op jit(solution)/shard_map/pallas_call | solution.py:435
  145.3 3.2 %copy.6 = bf16[512,2048]{1,0:T(8,128)(2,1)} copy(bf16[512,2048]{1,0:T(8,128)(2,1)} %shard_map.46) | data formatting | bytes 4194304

commit v4 on v3

--- a/solution.py
+++ b/solution.py
@@ -26,9 +26,9 @@
 
 
 def kernel(
-    rand, acts, queries, weight, out,
+    listed, acts, queries, weight, out,
     acts_v, wbuf, kv_send, kv, kvw, glob, before, after,
-    stage, pool, qx, acc, top, total, outbox, table, pairs,
+    stage, pool, qx, acc, top, total, outbox, table, pairs, rand,
     loc, wy_s, wy_r, wd_s, wd_r, wx_s, wx_r, kv_s, kv_r, q_s, q_r,
     m_s, m_r, st_s, pool_r, halo_s, halo_r, g_s, g_r, out_s, out_r, near_by,
 ):
@@ -74,6 +74,8 @@
         greet(at(0, dz, 0), y)
     for n in range(1, 8):
         greet(at(n // 2, 0, n % 2), y)
+    named = pltpu.make_async_copy(listed, rand, loc.at[3])
+    named.start()
     own_w = pltpu.make_async_copy(weight, pairs, loc.at[1])
     own_w.start()
     own_q = pltpu.make_async_copy(
@@ -105,6 +107,7 @@
     for dz in along:
         pl.semaphore_signal(near_by, inc=1, device_id=(at(0, dz, 0), y), device_id_type=pl.DeviceIdType.MESH)
     acts_in.wait()
+    named.wait()
 
     def project(head, dest, lead):
         def tile(t, _):
@@ -148,7 +151,7 @@
         found = jnp.int32(0)
         for r in range(RAND):
             for b in range(SHARD):
-                v = rand[r * N_CTX * SHARD + dst * SHARD + b]
+                v = rand[r, dst * SHARD + b]
                 found += jnp.where(v >> 4 == source, v & 15, 0)
         return found
 
@@ -279,20 +282,6 @@
         send_globals(head)
         multicast(n + 1, head)
 
-    @pl.when(c == 0)
-    def _():
-        to_glob.wait()
-
-    @pl.when(jnp.logical_and(on_line, c != 0))
-    def _():
-        landed(glob, g_s.at[0], g_r)
-
-    for holds, copies in tree:
-        @pl.when(holds)
-        def _():
-            for copy in copies():
-                copy.start()
-
     go(remote(kv.at[SHARD - 1], kvw.at[0], halo_s.at[0], halo_r.at[0], (c + 1) % N_CTX, y))
     go(remote(kv.at[0], kvw.at[SHARD + 1], halo_s.at[1], halo_r.at[1], (c + N_CTX - 1) % N_CTX, y))
     to_window = pltpu.make_async_copy(kv, kvw.at[pl.ds(1, SHARD)], loc.at[3])
@@ -303,6 +292,21 @@
                   qx.at[pl.ds(y * TOK, TOK)], q_s.at[n], q_r.at[n], c, head))
 
     pick("own", kv)
+
+    @pl.when(c == 0)
+    def _():
+        to_glob.wait()
+
+    @pl.when(jnp.logical_and(on_line, c != 0))
+    def _():
+        landed(glob, g_s.at[0], g_r)
+
+    for holds, copies in tree:
+        @pl.when(holds)
+        def _():
+            for copy in copies():
+                copy.start()
+
     for n, off in enumerate((0, *offs)):
         rows = pl.ds(peer(NY - off) * 4, 4)
         landed(before.at[rows], m_s.at[0, n], m_r.at[0, n])
@@ -371,7 +375,7 @@
 
     def finish(j, _):
         i = block_of(j)
-        chosen = [pool[rand[r * N_CTX * SHARD + c * SHARD + i] >> 4] for r in range(RAND)]
+        chosen = [pool[rand[r, c * SHARD + i] >> 4] for r in range(RAND)]
         keys = jnp.concatenate([b[:, 0:HEAD] for b in chosen], axis=0)
         values = jnp.concatenate([b[:, HEAD:ROW] for b in chosen], axis=0)
         for part in range(2):
@@ -432,10 +436,10 @@
     bf16, f32 = jnp.bfloat16, jnp.float32
     blocks = pltpu.VMEM((SHARD, BLOCK, ROW), bf16)
     dma = pltpu.SemaphoreType.DMA
-    return pl.pallas_call(
+    attended = pl.pallas_call(
         kernel,
         out_shape=jax.ShapeDtypeStruct((TOK, NY * QCOL), bf16),
-        in_specs=[pl.BlockSpec(memory_space=pltpu.SMEM)] + [pl.BlockSpec(memory_space=pl.ANY)] * 3,
+        in_specs=[pl.BlockSpec(memory_space=pl.ANY)] * 4,
         out_specs=pl.BlockSpec(memory_space=pl.ANY),
         scratch_shapes=[
             pltpu.VMEM((TOK, MODEL), bf16),
@@ -454,6 +458,7 @@
             pltpu.VMEM((NY * TOK, QCOL), bf16),
             pltpu.SMEM((N_CTX,), jnp.int32),
             pltpu.VMEM((2 * MODEL, HEAD), bf16),
+            pltpu.SMEM((RAND, N_CTX * SHARD), jnp.int32),
             dma((5,)), dma((6,)), dma((6,)), dma((2, 3)), dma((2, 3)), dma((3, 4)), dma((3, 4)),
             dma((3,)), dma((3,)), dma((3,)), dma((3,)),
             dma((2, 4)), dma((2, 4)), dma, dma, dma((2,)), dma((2,)), dma((14,)), dma,
@@ -465,7 +470,29 @@
         cost_estimate=pl.CostEstimate(
             flops=9 * 10**9, bytes_accessed=12 * 2**20, transcendentals=8 * 2**20
         ),
-    )(rand_blocks.T.reshape(-1), acts, queries, flat_weight)
+    )(rand_blocks.T, acts, queries, flat_weight)
+    parts = 8
+
+    def hand_over(source, dest, held, came, left):
+        rows = [pl.ds(n * TOK // parts, TOK // parts) for n in range(parts)]
+        reads = [pltpu.make_async_copy(source.at[r], held.at[r], came.at[n]) for n, r in enumerate(rows)]
+        writes = [pltpu.make_async_copy(held.at[r], dest.at[r], left.at[n]) for n, r in enumerate(rows)]
+        for copy in reads:
+            copy.start()
+        for read, write in zip(reads, writes):
+            read.wait()
+            write.start()
+        for copy in writes:
+            copy.wait()
+
+    return pl.pallas_call(
+        hand_over,
+        out_shape=jax.ShapeDtypeStruct((TOK, NY * QCOL), bf16),
+        in_specs=[pl.BlockSpec(memory_space=pl.ANY)],
+        out_specs=pl.BlockSpec(memory_space=pl.ANY),
+        scratch_shapes=[pltpu.VMEM((TOK, NY * QCOL), bf16), dma((parts,)), dma((parts,))],
+        compiler_params=pltpu.CompilerParams(vmem_limit_bytes=60 * 1024 * 1024),
+    )(attended)
 
 
 def solution(mesh):

time: 151 us -> 147 us (0.974)
  local copies, waits for them, and re-layouts: 4.48 us -> 0 us
    unnamed x1 -> x0, local copies, waits for them, and re-layouts: 3.16 us -> none
    pallas_call x0 -> x1, Pallas kernels: none -> 2.39 us  [shards(): pl.pallas_call(hand_over, out_shape=jax.ShapeDtypeStruct((TOK, NY * QCOL)...]
where the time goes in v4:
time: 147 us; the launch traced here: 145 us
  Pallas kernels  145 us (99%)
    pallas_call x1, Pallas kernels, shards(): pl.pallas_call(kernel, out_shape=jax.ShapeDtypeStruct((TOK, NY * QCOL), b...  143 us

profile of v4, /device:TPU:1, one launch (start us, length us, event | category | flops | bytes accessed | tf_op | source)
XLA Modules:
  0.0 145.4 jit_solution(18265639999543351901)
XLA Ops:
  0.0 143.0 %shard_map.46.source = bf16[512,2048]{1,0:T(8,128)(2,1)} custom-call(s32[3,1024]{1,0:T(4,128)} %bitcast.3, bf16[512,4096]{1,0:T(8,128)(2,1)} %acts.1, bf16[512,2048]{1,0:T(8,128)(2,1)} %queries.1, bf16[8192,128]{1,0:T(8,128)(2,1)} %bitcast.2), custom_call_target="tpu_custom_call" | custom-call | flops 8999999488 | bytes 12582912 | tf_op jit(solution)/shard_map/pallas_call | solution.py:439
  143.0 2.4 %shard_map.47 = bf16[512,2048]{1,0:T(8,128)(2,1)} custom-call(bf16[512,2048]{1,0:T(8,128)(2,1)} %shard_map.46.source), custom_call_target="tpu_custom_call" | custom-call | tf_op jit(solution)/shard_map/pallas_call | solution.py:488

commit v5 on v4

--- a/solution.py
+++ b/solution.py
@@ -74,10 +74,13 @@
         greet(at(0, dz, 0), y)
     for n in range(1, 8):
         greet(at(n // 2, 0, n % 2), y)
+    own_w = []
+    for n, slot in enumerate((1, 5, 6, 7)):
+        part = pl.ds((parity * 2 + k + n) % 4 * (2 * QUARTER), 2 * QUARTER)
+        own_w.append(pltpu.make_async_copy(weight.at[part], pairs.at[part], loc.at[slot]))
+        own_w[n].start()
     named = pltpu.make_async_copy(listed, rand, loc.at[3])
     named.start()
-    own_w = pltpu.make_async_copy(weight, pairs, loc.at[1])
-    own_w.start()
     own_q = pltpu.make_async_copy(
         queries.at[:, pl.ds(pl.multiple_of(y * QCOL, QCOL), QCOL)],
         qx.at[pl.ds(y * TOK, TOK)], loc.at[2],
@@ -85,7 +88,6 @@
     acts_in = pltpu.make_async_copy(acts, acts_v, loc.at[0])
     acts_in.start()
     own_q.start()
-    own_w.wait()
 
     line = lax.broadcasted_iota(jnp.int32, (2 * BLOCK, 2 * BLOCK), 0)
     place = lax.broadcasted_iota(jnp.int32, (2 * BLOCK, 2 * BLOCK), 1)
@@ -100,12 +102,19 @@
         wbuf[y, rows, HEAD:ROW] = parts[BLOCK:2 * BLOCK]
         return 0
 
-    lax.fori_loop(0, MODEL // BLOCK, set_apart, 0, unroll=4)
+    def set_quarter_apart(n):
+        own_w[n].wait()
+        start = (parity * 2 + k + n) % 4 * (QUARTER // BLOCK)
+        lax.fori_loop(0, QUARTER // BLOCK, lambda b, _: set_apart(start + b, 0), 0, unroll=4)
+
+    set_quarter_apart(0)
     pl.semaphore_wait(barrier, 16)
     for n, (off, rows) in enumerate(((1, first), (3, second), (1, second), (3, first))):
         go(remote(wbuf.at[y, rows], wbuf.at[y, rows], wy_s.at[n], wy_r.at[n], c, peer(off)))
     for dz in along:
         pl.semaphore_signal(near_by, inc=1, device_id=(at(0, dz, 0), y), device_id_type=pl.DeviceIdType.MESH)
+    for n in range(1, 4):
+        set_quarter_apart(n)
     acts_in.wait()
     named.wait()
 
@@ -459,7 +468,7 @@
             pltpu.SMEM((N_CTX,), jnp.int32),
             pltpu.VMEM((2 * MODEL, HEAD), bf16),
             pltpu.SMEM((RAND, N_CTX * SHARD), jnp.int32),
-            dma((5,)), dma((6,)), dma((6,)), dma((2, 3)), dma((2, 3)), dma((3, 4)), dma((3, 4)),
+            dma((8,)), dma((6,)), dma((6,)), dma((2, 3)), dma((2, 3)), dma((3, 4)), dma((3, 4)),
             dma((3,)), dma((3,)), dma((3,)), dma((3,)),
             dma((2, 4)), dma((2, 4)), dma, dma, dma((2,)), dma((2,)), dma((14,)), dma,
             dma((16,)), dma((16,)), pltpu.SemaphoreType.REGULAR,

time: 147 us -> 148 us (level); the launches traced: 145 us -> 148 us
  Pallas kernels: 145 us -> 148 us
    pallas_call x1, Pallas kernels: 143 us -> 146 us  [shards(): pl.pallas_call(kernel, out_shape=jax.ShapeDtypeStruct((TOK, NY * QCOL), b...]
where the time goes in v5:
time: 148 us
  Pallas kernels  148 us (100%)
    pallas_call x1, Pallas kernels, shards(): pl.pallas_call(kernel, out_shape=jax.ShapeDtypeStruct((TOK, NY * QCOL), b...  146 us

profile of v5, /device:TPU:1, one launch (start us, length us, event | category | flops | bytes accessed | tf_op | source)
XLA Modules:
  0.0 148.1 jit_solution(2420883284045382776)
XLA Ops:
  0.0 145.7 %shard_map.46.source = bf16[512,2048]{1,0:T(8,128)(2,1)} custom-call(s32[3,1024]{1,0:T(4,128)} %bitcast.3, bf16[512,4096]{1,0:T(8,128)(2,1)} %acts.1, bf16[512,2048]{1,0:T(8,128)(2,1)} %queries.1, bf16[8192,128]{1,0:T(8,128)(2,1)} %bitcast.2), custom_call_target="tpu_custom_call" | custom-call | flops 8999999488 | bytes 12582912 | tf_op jit(solution)/shard_map/pallas_call | solution.py:448
  145.7 2.4 %shard_map.47 = bf16[512,2048]{1,0:T(8,128)(2,1)} custom-call(bf16[512,2048]{1,0:T(8,128)(2,1)} %shard_map.46.source), custom_call_target="tpu_custom_call" | custom-call | tf_op jit(solution)/shard_map/pallas_call | solution.py:497

commit v6 on v4

--- a/solution.py
+++ b/solution.py
@@ -138,12 +138,12 @@
         "own": (c, 0, 1, 8, in_plane),
         "below 3": (below, 7, 0, 4, lambda n: at(n, 3, 0)),
         "above 3": (above, 11, 0, 4, lambda n: at(n, NZ - 3, 1)),
+        "below": (below, 47, 1, 8, in_plane),
+        "above": (above, 54, 1, 8, in_plane),
         "below 2": (below, 15, 0, 8, lambda n: at(n // 2, 2, n % 2)),
         "above 2": (above, 23, 0, 8, lambda n: at(n // 2, NZ - 2, n % 2)),
         "below 1": (below, 31, 0, 8, lambda n: at(n // 2, 1, n % 2)),
         "above 1": (above, 39, 0, 8, lambda n: at(n // 2, NZ - 1, n % 2)),
-        "below": (below, 47, 1, 8, in_plane),
-        "above": (above, 54, 1, 8, in_plane),
     }
     keep = {"own": 61, "below": 62, "above": 63}
 

time: 147 us -> 147 us (level)
  no operation moved by 1% of the time
where the time goes in v6:
time: 147 us; the launch traced here: 145 us
  Pallas kernels  145 us (99%)
    pallas_call x1, Pallas kernels, shards(): pl.pallas_call(kernel, out_shape=jax.ShapeDtypeStruct((TOK, NY * QCOL), b...  143 us

profile of v6, /device:TPU:1, one launch (start us, length us, event | category | flops | bytes accessed | tf_op | source)
XLA Modules:
  0.0 145.4 jit_solution(5238721258855781958)
XLA Ops:
  0.0 143.0 %shard_map.46.source = bf16[512,2048]{1,0:T(8,128)(2,1)} custom-call(s32[3,1024]{1,0:T(4,128)} %bitcast.3, bf16[512,4096]{1,0:T(8,128)(2,1)} %acts.1, bf16[512,2048]{1,0:T(8,128)(2,1)} %queries.1, bf16[8192,128]{1,0:T(8,128)(2,1)} %bitcast.2), custom_call_target="tpu_custom_call" | custom-call | flops 8999999488 | bytes 12582912 | tf_op jit(solution)/shard_map/pallas_call | solution.py:439
  143.0 2.4 %shard_map.47 = bf16[512,2048]{1,0:T(8,128)(2,1)} custom-call(bf16[512,2048]{1,0:T(8,128)(2,1)} %shard_map.46.source), custom_call_target="tpu_custom_call" | custom-call | tf_op jit(solution)/shard_map/pallas_call | solution.py:488
